TPU v7x, 32 devices: a whole 2x2x4 slice. The times are simulated.
32 devices in a mesh: parts: 2 (over y), cols: 4 (over z), rows: 2 (over x), rep: 2 (over core).
Axes of the slice: x: 2, y: 2, z: 4, core: 2. Of those that a mesh axis runs over, the one named last changes fastest.
Arguments:
- sources: float32 [4096, 64], P(('parts', 'rows')), parts along dimension 0, may hold values from -11 to 11
- source_mass: float32 [4096], P(('parts', 'rows')), parts along dimension 0, may hold values from 0.2 to 5
- targets: float32 [4096, 64], P(('parts', 'cols', 'rep')), parts along dimension 0, may hold values from -6 to 6
- target_mass: float32 [4096], P(('parts', 'cols', 'rep')), parts along dimension 0, may hold values from 0.2 to 5
- fate_panel: float32 [4096, 64], P(('parts', 'cols', 'rep')), parts along dimension 0, may hold values from 0 to 1
Outputs:
- f_pot: float32 [4096], P(('parts', 'rows')), parts along dimension 0
- g_pot: float32 [4096], P(('parts', 'cols', 'rep')), parts along dimension 0
- fate_rows: float32 [4096, 64], P(('parts', 'rows', 'cols', 'rep')), parts along dimension 0
There are 2 independent parts, one for each index of `parts`. A program takes and returns all parts, laid end to end along the dimension named above; each array names one. Nothing has to cross between parts.
All inputs are finite; a program needn't handle non-finite values.
Results may differ from a plain program's by a relative error of at most 0.0003.
Values sent between devices are 32-bit elements; how exact they have to be, the bound alone decides.
A program may use at most 64 MiB of HBM per device.

v0:
```python
import math

import jax
import jax.numpy as jnp
from jax import lax
from jax.sharding import PartitionSpec as P

ITERS = 8


entropic = 0.1
relaxed = 1.0 / 1.1


def pair_cost(lhs_rows, lhs_sq, rhs_rows, rhs_sq):
    products = lax.dot_general(
        lhs_rows,
        rhs_rows,
        (((1,), (1,)), ((), ())),
        precision=lax.Precision.HIGHEST,
        preferred_element_type=jnp.float32,
    )
    return (lhs_sq[:, None] + rhs_sq[None, :] - 2.0 * products) / lhs_rows.shape[1]


def row_potential(maxima, totals):
    whole_peak = lax.pmax(maxima, ("cols", "rep"))
    whole_total = lax.psum(totals * jnp.exp(maxima - whole_peak), ("cols", "rep"))
    return -relaxed * entropic * (whole_peak + jnp.log(whole_total))


def col_potential(maxima, totals):
    whole_peak = lax.pmax(maxima, "rows")
    whole_total = lax.psum(totals * jnp.exp(maxima - whole_peak), "rows")
    return -relaxed * entropic * (whole_peak + jnp.log(whole_total))


def body(sources, source_mass, targets, target_mass, fate_panel):
    src_count = sources.shape[0]
    tgt_count = targets.shape[0]
    feature_dim = sources.shape[1]
    all_sources = src_count * lax.axis_size("rows")
    all_targets = tgt_count * lax.axis_size(("cols", "rep"))
    log_a = jnp.log(source_mass / all_sources)
    log_b = jnp.log(target_mass / all_targets)
    src_sq = jnp.sum(sources * sources, axis=1)
    tgt_sq = jnp.sum(targets * targets, axis=1)
    row_size = math.gcd(src_count, 512)
    block_count = src_count // row_size
    src_blocks = sources.reshape(block_count, row_size, feature_dim)
    sq_blocks = src_sq.reshape(block_count, row_size)
    loga_blocks = log_a.reshape(block_count, row_size)

    def row_scores(packed, g_pot):
        return (
            log_b[None, :]
            + (g_pot[None, :] - pair_cost(packed[0], packed[1], targets, tgt_sq)) / entropic
        )

    g_pot = jnp.zeros((tgt_count,), jnp.float32)
    f_pot = jnp.zeros((src_count,), jnp.float32)
    for iteration in range(ITERS):

        def row_per_block(packed):
            scores = row_scores(packed, g_pot)
            maxima = jnp.max(scores, axis=1)
            return (maxima, jnp.sum(jnp.exp(scores - maxima[:, None]), axis=1))

        maxima, row_totals = lax.map(row_per_block, (src_blocks, sq_blocks))
        maxima, totals = (maxima.reshape(src_count), row_totals.reshape(src_count))
        f_pot = row_potential(maxima, totals)
        f_blocks = f_pot.reshape(block_count, row_size)

        def col_per_block(running, packed):
            scores = (
                packed[2][:, None]
                + (packed[3][:, None] - pair_cost(packed[0], packed[1], targets, tgt_sq)) / entropic
            )
            highest = jnp.maximum(running[0], jnp.max(scores, axis=0))
            totals = running[1] * jnp.exp(running[0] - highest) + jnp.sum(
                jnp.exp(scores - highest[None, :]), axis=0
            )
            return ((highest, totals), None)

        initial = (
            jnp.full((tgt_count,), -jnp.inf, jnp.float32),
            jnp.zeros((tgt_count,), jnp.float32),
        )
        running, unused = lax.scan(
            col_per_block, initial, (src_blocks, sq_blocks, loga_blocks, f_blocks)
        )
        maxima, totals = running
        g_pot = col_potential(maxima, totals)

    def fate_block(packed):
        scores = row_scores(packed, g_pot)
        maxima = jnp.max(scores, axis=1)
        weights = jnp.exp(scores - maxima[:, None])
        totals = jnp.sum(weights, axis=1)
        weighted = jnp.dot(
            weights, fate_panel, precision=lax.Precision.HIGHEST, preferred_element_type=jnp.float32
        )
        return (maxima, totals, weighted)

    maxima, totals, weighted = lax.map(fate_block, (src_blocks, sq_blocks))
    maxima = maxima.reshape(src_count)
    totals = totals.reshape(src_count)
    weighted = weighted.reshape(src_count, fate_panel.shape[1])
    whole_peak = lax.pmax(maxima, ("cols", "rep"))
    factor = jnp.exp(maxima - whole_peak)
    part_weighted, part_total = (
        lax.psum_scatter(
            weighted * factor[:, None], ("cols", "rep"), scatter_dimension=0, tiled=True
        ),
        lax.psum_scatter(totals * factor, ("cols", "rep"), scatter_dimension=0, tiled=True),
    )
    fate_rows = part_weighted / part_total[:, None]
    return (f_pot, g_pot, fate_rows)


def solution(mesh):
    in_specs = (
        P(("parts", "rows"), None),
        P(("parts", "rows")),
        P(("parts", "cols", "rep"), None),
        P(("parts", "cols", "rep")),
        P(("parts", "cols", "rep"), None),
    )
    out_specs = (
        P(("parts", "rows")),
        P(("parts", "cols", "rep")),
        P(("parts", "rows", "cols", "rep"), None),
    )
    return jax.shard_map(body, mesh=mesh, in_specs=in_specs, out_specs=out_specs, check_vma=False)
```

profile of v0, /device:TPU:0, one launch (start us, length us, event | category | flops | bytes accessed | tf_op | source)
XLA Modules:
  0.0 398.9 jit_solution(12835680924114328844)
XLA Ops:
  11.3 18.1 %pmax.119 = f32[1024]{0:T(1024)S(1)} all-reduce(f32[1024]{0:T(1024)S(1)} %bitcast.428), channel_id=1, replica_groups=mesh['parts'=2,'cols'=4,'rows'=2,'rep'=2] {'cols','rep'}, use_global_device_ids=true, to_apply=%region_6.7 | all-reduce | flops 1024 | bytes 8192 | tf_op jit(solution)/shard_map/pmax | solution.py:27
  29.4 13.6 %psum.112 = f32[1024]{0:T(1024)S(1)} all-reduce(f32[1024]{0:T(1024)S(1)} %exponential_multiply_fusion.7), channel_id=1, replica_groups=mesh['parts'=2,'cols'=4,'rows'=2,'rep'=2] {'cols','rep'}, use_global_device_ids=true, to_apply=%region_7.8 | all-reduce | flops 1024 | bytes 8192 | tf_op jit(solution)/shard_map/psum | solution.py:28
  44.8 4.9 %pmax.120 = f32[256]{0:T(256)S(1)} all-reduce(f32[256]{0:T(256)S(1)} %get-tuple-element.827), channel_id=1, replica_groups=mesh['parts'=2,'cols'=4,'rows'=2,'rep'=2] {'rows'}, use_global_device_ids=true, to_apply=%region_12.13 | all-reduce | flops 256 | bytes 2048 | tf_op jit(solution)/shard_map/pmax | solution.py:33
  49.7 4.9 %psum.113 = f32[256]{0:T(256)S(1)} all-reduce(f32[256]{0:T(256)S(1)} %exponential_multiply_fusion.15), channel_id=1, replica_groups=mesh['parts'=2,'cols'=4,'rows'=2,'rep'=2] {'rows'}, use_global_device_ids=true, to_apply=%region_13.14 | all-reduce | flops 256 | bytes 2048 | tf_op jit(solution)/shard_map/psum | solution.py:34
  56.6 13.6 %pmax.121 = f32[1024]{0:T(1024)S(1)} all-reduce(f32[1024]{0:T(1024)S(1)} %bitcast.430), channel_id=1, replica_groups=mesh['parts'=2,'cols'=4,'rows'=2,'rep'=2] {'cols','rep'}, use_global_device_ids=true, to_apply=%region_18.19 | all-reduce | flops 1024 | bytes 8192 | tf_op jit(solution)/shard_map/pmax | solution.py:27
  70.2 13.6 %psum.114 = f32[1024]{0:T(1024)S(1)} all-reduce(f32[1024]{0:T(1024)S(1)} %exponential_multiply_fusion.6), channel_id=1, replica_groups=mesh['parts'=2,'cols'=4,'rows'=2,'rep'=2] {'cols','rep'}, use_global_device_ids=true, to_apply=%region_19.20 | all-reduce | flops 1024 | bytes 8192 | tf_op jit(solution)/shard_map/psum | solution.py:28
  85.6 4.9 %pmax.122 = f32[256]{0:T(256)S(1)} all-reduce(f32[256]{0:T(256)S(1)} %get-tuple-element.831), channel_id=1, replica_groups=mesh['parts'=2,'cols'=4,'rows'=2,'rep'=2] {'rows'}, use_global_device_ids=true, to_apply=%region_24.25 | all-reduce | flops 256 | bytes 2048 | tf_op jit(solution)/shard_map/pmax | solution.py:33
  90.5 4.9 %psum.115 = f32[256]{0:T(256)S(1)} all-reduce(f32[256]{0:T(256)S(1)} %exponential_multiply_fusion.14), channel_id=1, replica_groups=mesh['parts'=2,'cols'=4,'rows'=2,'rep'=2] {'rows'}, use_global_device_ids=true, to_apply=%region_25.26 | all-reduce | flops 256 | bytes 2048 | tf_op jit(solution)/shard_map/psum | solution.py:34
  97.4 13.6 %pmax.123 = f32[1024]{0:T(1024)S(1)} all-reduce(f32[1024]{0:T(1024)S(1)} %bitcast.432), channel_id=1, replica_groups=mesh['parts'=2,'cols'=4,'rows'=2,'rep'=2] {'cols','rep'}, use_global_device_ids=true, to_apply=%region_30.31 | all-reduce | flops 1024 | bytes 8192 | tf_op jit(solution)/shard_map/pmax | solution.py:27
  111.0 13.6 %psum.116 = f32[1024]{0:T(1024)S(1)} all-reduce(f32[1024]{0:T(1024)S(1)} %exponential_multiply_fusion.5), channel_id=1, replica_groups=mesh['parts'=2,'cols'=4,'rows'=2,'rep'=2] {'cols','rep'}, use_global_device_ids=true, to_apply=%region_31.32 | all-reduce | flops 1024 | bytes 8192 | tf_op jit(solution)/shard_map/psum | solution.py:28
  126.4 4.9 %pmax.124 = f32[256]{0:T(256)S(1)} all-reduce(f32[256]{0:T(256)S(1)} %get-tuple-element.835), channel_id=1, replica_groups=mesh['parts'=2,'cols'=4,'rows'=2,'rep'=2] {'rows'}, use_global_device_ids=true, to_apply=%region_36.37 | all-reduce | flops 256 | bytes 2048 | tf_op jit(solution)/shard_map/pmax | solution.py:33
  138.2 13.6 %pmax.125 = f32[1024]{0:T(1024)S(1)} all-reduce(f32[1024]{0:T(1024)S(1)} %bitcast.434), channel_id=1, replica_groups=mesh['parts'=2,'cols'=4,'rows'=2,'rep'=2] {'cols','rep'}, use_global_device_ids=true, to_apply=%region_42.43 | all-reduce | flops 1024 | bytes 8192 | tf_op jit(solution)/shard_map/pmax | solution.py:27
  151.8 13.6 %psum.118 = f32[1024]{0:T(1024)S(1)} all-reduce(f32[1024]{0:T(1024)S(1)} %exponential_multiply_fusion.4), channel_id=1, replica_groups=mesh['parts'=2,'cols'=4,'rows'=2,'rep'=2] {'cols','rep'}, use_global_device_ids=true, to_apply=%region_43.44 | all-reduce | flops 1024 | bytes 8192 | tf_op jit(solution)/shard_map/psum | solution.py:28
  167.2 4.9 %pmax.126 = f32[256]{0:T(256)S(1)} all-reduce(f32[256]{0:T(256)S(1)} %get-tuple-element.839), channel_id=1, replica_groups=mesh['parts'=2,'cols'=4,'rows'=2,'rep'=2] {'rows'}, use_global_device_ids=true, to_apply=%region_48.49 | all-reduce | flops 256 | bytes 2048 | tf_op jit(solution)/shard_map/pmax | solution.py:33
  172.1 4.9 %psum.119 = f32[256]{0:T(256)S(1)} all-reduce(f32[256]{0:T(256)S(1)} %exponential_multiply_fusion.12), channel_id=1, replica_groups=mesh['parts'=2,'cols'=4,'rows'=2,'rep'=2] {'rows'}, use_global_device_ids=true, to_apply=%region_49.50 | all-reduce | flops 256 | bytes 2048 | tf_op jit(solution)/shard_map/psum | solution.py:34
  179.0 13.6 %pmax.127 = f32[1024]{0:T(1024)S(1)} all-reduce(f32[1024]{0:T(1024)S(1)} %bitcast.436), channel_id=1, replica_groups=mesh['parts'=2,'cols'=4,'rows'=2,'rep'=2] {'cols','rep'}, use_global_device_ids=true, to_apply=%region_54.55 | all-reduce | flops 1024 | bytes 8192 | tf_op jit(solution)/shard_map/pmax | solution.py:27
  192.7 13.6 %psum.120 = f32[1024]{0:T(1024)S(1)} all-reduce(f32[1024]{0:T(1024)S(1)} %exponential_multiply_fusion.3), channel_id=1, replica_groups=mesh['parts'=2,'cols'=4,'rows'=2,'rep'=2] {'cols','rep'}, use_global_device_ids=true, to_apply=%region_55.56 | all-reduce | flops 1024 | bytes 8192 | tf_op jit(solution)/shard_map/psum | solution.py:28
  208.0 4.9 %pmax.128 = f32[256]{0:T(256)S(1)} all-reduce(f32[256]{0:T(256)S(1)} %get-tuple-element.843), channel_id=1, replica_groups=mesh['parts'=2,'cols'=4,'rows'=2,'rep'=2] {'rows'}, use_global_device_ids=true, to_apply=%region_60.61 | all-reduce | flops 256 | bytes 2048 | tf_op jit(solution)/shard_map/pmax | solution.py:33
  212.9 5.1 %psum.121 = f32[256]{0:T(256)S(1)} all-reduce(f32[256]{0:T(256)S(1)} %exponential_multiply_fusion.11), channel_id=1, replica_groups=mesh['parts'=2,'cols'=4,'rows'=2,'rep'=2] {'rows'}, use_global_device_ids=true, to_apply=%region_61.62 | all-reduce | flops 256 | bytes 2048 | tf_op jit(solution)/shard_map/psum | solution.py:34
  220.0 13.6 %pmax.129 = f32[1024]{0:T(1024)S(1)} all-reduce(f32[1024]{0:T(1024)S(1)} %bitcast.438), channel_id=1, replica_groups=mesh['parts'=2,'cols'=4,'rows'=2,'rep'=2] {'cols','rep'}, use_global_device_ids=true, to_apply=%region_66.67 | all-reduce | flops 1024 | bytes 8192 | tf_op jit(solution)/shard_map/pmax | solution.py:27
  233.6 13.6 %psum.122 = f32[1024]{0:T(1024)S(1)} all-reduce(f32[1024]{0:T(1024)S(1)} %exponential_multiply_fusion.2), channel_id=1, replica_groups=mesh['parts'=2,'cols'=4,'rows'=2,'rep'=2] {'cols','rep'}, use_global_device_ids=true, to_apply=%region_67.68 | all-reduce | flops 1024 | bytes 8192 | tf_op jit(solution)/shard_map/psum | solution.py:28
  249.0 4.9 %pmax.130 = f32[256]{0:T(256)S(1)} all-reduce(f32[256]{0:T(256)S(1)} %get-tuple-element.847), channel_id=1, replica_groups=mesh['parts'=2,'cols'=4,'rows'=2,'rep'=2] {'rows'}, use_global_device_ids=true, to_apply=%region_72.73 | all-reduce | flops 256 | bytes 2048 | tf_op jit(solution)/shard_map/pmax | solution.py:33
  260.8 13.6 %pmax.131 = f32[1024]{0:T(1024)S(1)} all-reduce(f32[1024]{0:T(1024)S(1)} %bitcast.440), channel_id=1, replica_groups=mesh['parts'=2,'cols'=4,'rows'=2,'rep'=2] {'cols','rep'}, use_global_device_ids=true, to_apply=%region_78.79 | all-reduce | flops 1024 | bytes 8192 | tf_op jit(solution)/shard_map/pmax | solution.py:27
  274.4 13.6 %psum.124 = f32[1024]{0:T(1024)S(1)} all-reduce(f32[1024]{0:T(1024)S(1)} %exponential_multiply_fusion.1), channel_id=1, replica_groups=mesh['parts'=2,'cols'=4,'rows'=2,'rep'=2] {'cols','rep'}, use_global_device_ids=true, to_apply=%region_79.80 | all-reduce | flops 1024 | bytes 8192 | tf_op jit(solution)/shard_map/psum | solution.py:28
  289.8 4.9 %pmax.132 = f32[256]{0:T(256)S(1)} all-reduce(f32[256]{0:T(256)S(1)} %get-tuple-element.851), channel_id=1, replica_groups=mesh['parts'=2,'cols'=4,'rows'=2,'rep'=2] {'rows'}, use_global_device_ids=true, to_apply=%region_84.85 | all-reduce | flops 256 | bytes 2048 | tf_op jit(solution)/shard_map/pmax | solution.py:33
  301.6 13.6 %pmax.133 = f32[1024]{0:T(1024)S(1)} all-reduce(f32[1024]{0:T(1024)S(1)} %bitcast.442), channel_id=1, replica_groups=mesh['parts'=2,'cols'=4,'rows'=2,'rep'=2] {'cols','rep'}, use_global_device_ids=true, to_apply=%region_90.91 | all-reduce | flops 1024 | bytes 8192 | tf_op jit(solution)/shard_map/pmax | solution.py:27
  315.3 13.6 %psum.126 = f32[1024]{0:T(1024)S(1)} all-reduce(f32[1024]{0:T(1024)S(1)} %exponential_multiply_fusion), channel_id=1, replica_groups=mesh['parts'=2,'cols'=4,'rows'=2,'rep'=2] {'cols','rep'}, use_global_device_ids=true, to_apply=%region_91.92 | all-reduce | flops 1024 | bytes 8192 | tf_op jit(solution)/shard_map/psum | solution.py:28
  331.2 4.9 %pmax.134 = f32[256]{0:T(256)S(1)} all-reduce(f32[256]{0:T(256)S(1)} %get-tuple-element.855), channel_id=1, replica_groups=mesh['parts'=2,'cols'=4,'rows'=2,'rep'=2] {'rows'}, use_global_device_ids=true, to_apply=%region_96.97 | all-reduce | flops 256 | bytes 2048 | tf_op jit(solution)/shard_map/pmax | solution.py:33
  341.1 5.7 %while.222 = (s32[]{:T(128)}, f32[2,512]{1,0:T(2,128)S(1)}, f32[2,512]{1,0:T(2,128)S(1)}, f32[2,512,64]{1,0,2:T(2,128)S(1)}, f32[256]{0:T(256)S(1)}, /*index=5*/...) while((s32[]{:T(128)}, f32[2,512]{1,0:T(2,128)S(1)}, ...), condition=%wide.region_101.102_spmd, body=%wide.region_98.101_spmd.sunk | while | flops 202767360 | bytes 2647193 | solution.py:105
  347.4 13.6 %pmax.135 = f32[1024]{0:T(1024)S(1)} all-reduce(f32[1024]{0:T(1024)S(1)} %bitcast.426), channel_id=1, replica_groups=mesh['parts'=2,'cols'=4,'rows'=2,'rep'=2] {'cols','rep'}, use_global_device_ids=true, to_apply=%region_102.103 | all-reduce | flops 1024 | bytes 8192 | tf_op jit(solution)/shard_map/pmax | solution.py:109
  363.7 13.6 %all-reduce = f32[1024]{0:T(1024)S(1)} all-reduce(f32[1024]{0:T(1024)S(1)} %get-tuple-element.1408), channel_id=3, replica_groups=mesh['parts'=2,'cols'=4,'rows'=2,'rep'=2] {'cols','rep'}, use_global_device_ids=true, to_apply=%region_104.105.clone | all-reduce | flops 1024 | bytes 8192
  377.4 13.3 %reduce-scatter.2.cloned.1.call-done = f32[128,64]{0,1:T(8,128)} async-done(((f32[1024,64]{0,1:T(8,128)}), f32[128,64]{0,1:T(8,128)}) %reduce-scatter.2.cloned.1.call-update) | async-done | bytes 32784 | tf_op jit(solution)/shard_map/reduce_scatter | solution.py:112
  (352 shorter events, 89.6 us)
Async XLA Ops:
  7.2 1.2 copy-start.1
  7.2 383.5 %reduce-scatter.2.cloned.1.call-start = ((), (), s32[]{:S(2)}) async-start(), calls=%async_computation.1 | async-start | bytes 294912 | tf_op jit(solution)/shard_map/reduce_scatter | solution.py:112
  8.4 1.0 copy-start.2
  8.6 0.7 copy-start.4
  8.6 0.7 copy-start.6
  328.9 0.6 copy-start.3
  329.5 11.6 %copy-start = (f32[256,64]{0,1:T(8,128)S(1)}, f32[256,64]{0,1:T(8,128)}, u32[]{:S(2)}) copy-start(f32[256,64]{0,1:T(8,128)} %param.43) | copy-start | bytes 196612
  346.8 0.6 copy-start.5
  361.8 0.7 copy-start.7
Sparse Core Ops, SparseCore 0:
  361.9 28.7 reduce-scatter.1
where the time goes:
time: 400 us; the launch traced here: 399 us
  blocking collectives  328 us (82%)
  matrix products  24.7 us (6%)
  between operations  15.2 us (4%)
  waiting for transfers between devices  13.3 us (3%)
  local copies, waits for them, and re-layouts  8.2 us (2%)
  other arithmetic  7.79 us (2%)
    pmax x8, blocking collectives, row_potential(): whole_peak = lax.pmax(maxima, ('cols', 'rep'))  113 us
    psum x8, blocking collectives, row_potential(): lax.psum(totals * jnp.exp(maxima - whole_peak), ('cols', 'rep'))  109 us
    psum x8, blocking collectives, col_potential(): whole_total = lax.psum(totals * jnp.exp(maxima - whole_peak), 'rows')  39.6 us
    pmax x8, blocking collectives, col_potential(): whole_peak = lax.pmax(maxima, 'rows')  39.5 us
    dot_general x34, matrix products, pair_cost(): lax.dot_general(lhs_rows, rhs_rows, (((1,), (1,)), ((), ())), precision=l...  23.7 us
    unnamed x1, blocking collectives  13.6 us
    pmax x1, blocking collectives, body(): whole_peak = lax.pmax(maxima, ('cols', 'rep'))  13.6 us
    reduce_scatter x1, waiting for transfers between devices, body(): lax.psum_scatter(weighted * factor[:, None], ('cols', 'rep'), scatter_dim...  13.3 us
  transfers between devices with their start and end apart: 1, of which 1 were waited for; matrix products, arithmetic and copies ran while one was open for 0% of the time, Pallas kernels for 0%

commit v1 on v0

v1 whole, which is shorter than its diff:
```python
import functools
import math

import jax
import jax.numpy as jnp
from jax import lax
from jax.experimental import pallas as pl
from jax.experimental.pallas import tpu as pltpu
from jax.sharding import PartitionSpec as P

ITERS = 8
LANES = 128
CHUNK = 8
entropic = 0.1
relaxed = 1.0 / 1.1
HIGHEST = lax.Precision.HIGHEST
MESH = pl.DeviceIdType.MESH


def peak_total(x):
    peak = jnp.max(x, axis=0)
    return peak, jnp.sum(jnp.exp2(x - peak[None]), axis=0)


def kernel(
    sizes, src_ref, smass_ref, tgt_ref, tmass_ref, fate_ref,
    f_ref, g_ref, out_ref,
    tt, ft, scores, log_b, g_scaled, log_a, f_scaled, row_peak, row_total, parts, f_parts,
    tt_send, tt_recv, fwd_send, fwd_recv, ft_send, ft_recv, ex_send, ex_recv, f_send, f_recv,
):
    X, C, R, src_count, tgt_count, dim, fates = sizes
    rows = src_count // R
    own = src_count // (C * R)
    blocks = C * R * tgt_count // LANES
    chunks = blocks // CHUNK
    per = tgt_count // LANES
    groups = rows // 8
    peers = X * R
    x_id, c_id, r_id = lax.axis_index("rows"), lax.axis_index("cols"), lax.axis_index("rep")
    me = x_id * R + r_id
    all_sources, all_targets = src_count * X, tgt_count * C * R
    unit = math.log2(math.e) / (dim * entropic)

    def peer(step):
        other = lax.rem(me + step, peers)
        return {"rows": other // R, "rep": lax.rem(other, R)}

    def col_of(step):
        return lax.rem(c_id + step, C)

    def rep_of(step):
        return lax.rem(r_id + step, R)

    barrier = pltpu.get_barrier_semaphore()
    for step in range(1, peers):
        pl.semaphore_signal(barrier, inc=1, device_id=peer(step), device_id_type=MESH)
    for step in range(1, C):
        for turn in range(R):
            pl.semaphore_signal(
                barrier, inc=1, device_id={"cols": col_of(step), "rep": rep_of(turn)},
                device_id_type=MESH,
            )

    both = jnp.concatenate([tgt_ref[...], fate_ref[...]], axis=1)
    for k in range(per):
        turned = both[k * LANES:(k + 1) * LANES].T
        tt[c_id, r_id, 0:dim, k * LANES:(k + 1) * LANES] = turned[:dim]
        ft[c_id, r_id, :, k * LANES:(k + 1) * LANES] = turned[dim:]
    tt[c_id, r_id, dim:dim + 8, :] = jnp.broadcast_to(
        jnp.log2(tmass_ref[...] / all_targets), (8, tgt_count)
    )

    pl.semaphore_wait(barrier, peers - 1 + (C - 1) * R)

    def tt_copy(step):
        return pltpu.make_async_remote_copy(
            src_ref=tt.at[c_id, r_id], dst_ref=tt.at[c_id, r_id],
            send_sem=tt_send.at[step], recv_sem=tt_recv.at[c_id],
            device_id={"cols": col_of(step)}, device_id_type=MESH,
        )

    def fwd_copy(col, turn):
        return pltpu.make_async_remote_copy(
            src_ref=tt.at[col, r_id], dst_ref=tt.at[col, r_id],
            send_sem=fwd_send.at[col, turn], recv_sem=fwd_recv.at[col, r_id],
            device_id={"rep": rep_of(turn)}, device_id_type=MESH,
        )

    def ft_copy(step, turn):
        return pltpu.make_async_remote_copy(
            src_ref=ft.at[c_id, r_id], dst_ref=ft.at[c_id, r_id],
            send_sem=ft_send.at[step, turn], recv_sem=ft_recv.at[c_id, r_id],
            device_id={"cols": col_of(step), "rep": rep_of(turn)}, device_id_type=MESH,
        )

    def tt_arrived(col):
        pltpu.make_async_remote_copy(
            src_ref=tt.at[col, r_id], dst_ref=tt.at[col, r_id],
            send_sem=tt_send.at[0], recv_sem=tt_recv.at[col],
            device_id={"cols": col}, device_id_type=MESH,
        ).wait_recv()

    def fwd_arrived(col, rep):
        pltpu.make_async_remote_copy(
            src_ref=tt.at[col, rep], dst_ref=tt.at[col, rep],
            send_sem=fwd_send.at[col, 0], recv_sem=fwd_recv.at[col, rep],
            device_id={"rep": rep}, device_id_type=MESH,
        ).wait_recv()

    def ft_arrived(col, rep):
        pltpu.make_async_remote_copy(
            src_ref=ft.at[col, rep], dst_ref=ft.at[col, rep],
            send_sem=ft_send.at[0, 0], recv_sem=ft_recv.at[col, rep],
            device_id={"cols": col, "rep": rep}, device_id_type=MESH,
        ).wait_recv()

    for step in range(1, C):
        tt_copy(step).start()
    for turn in range(1, R):
        fwd_copy(c_id, turn).start()
    for step in list(range(1, C)) + [0]:
        for turn in range(R):
            if step or turn:
                ft_copy(step, turn).start()

    first = pl.multiple_of(r_id * rows, rows)
    first_own = pl.multiple_of((c_id * R + r_id) * own, own)
    mine = jnp.concatenate([src_ref[pl.ds(first, rows), :], src_ref[pl.ds(first_own, own), :]], axis=0)
    src_sq = jnp.sum(mine * mine, axis=1, keepdims=True) * unit
    mine = mine * (2.0 * unit)

    def fill(col, rep):
        block = tt[col, rep, 0:dim, :]
        products = jnp.dot(mine, block, precision=HIGHEST, preferred_element_type=jnp.float32)
        values = products - (src_sq + jnp.sum(block * block, axis=0, keepdims=True) * unit)
        for k in range(per):
            at = (col * R + rep) * per + k
            scores[at] = values[:, k * LANES:(k + 1) * LANES]
            level = tt[col, rep, dim:dim + 8, k * LANES:(k + 1) * LANES]
            log_b[at] = level
            g_scaled[at] = level

    fill(c_id, r_id)
    for k in range(rows // LANES):
        level = jnp.log2(smass_ref[r_id, k:k + 1, :] / all_sources)
        log_a[k * LANES:(k + 1) * LANES, :] = jnp.broadcast_to(level, (LANES, LANES)).T
    for turn in range(1, R):
        fwd_arrived(c_id, rep_of(turn))
        fill(c_id, rep_of(turn))
    for step in range(1, C):
        tt_arrived(col_of(step))
        for turn in range(1, R):
            fwd_copy(col_of(step), turn).start()
        fill(col_of(step), r_id)
    for step in range(1, C):
        for turn in range(1, R):
            fwd_arrived(col_of(step), rep_of(turn))
            fill(col_of(step), rep_of(turn))

    def row_chunk(chunk):
        def row_group(group, carry):
            at = pl.multiple_of(group * 8, 8)
            base = chunk * CHUNK
            x = scores[pl.ds(base, CHUNK), pl.ds(at, 8), :] + g_scaled[pl.ds(base, CHUNK)]
            peak, total = peak_total(x)
            row_peak[chunk, pl.ds(at, 8), :] = peak
            row_total[chunk, pl.ds(at, 8), :] = total
            return carry

        lax.fori_loop(0, groups, row_group, 0, unroll=4)

    def row_finish():
        def some(k, carry):
            at = pl.multiple_of(k * 64, 64)
            peaks = row_peak[:, pl.ds(at, 64), :]
            top = jnp.max(jnp.max(peaks, axis=0), axis=1, keepdims=True)
            totals = jnp.sum(row_total[:, pl.ds(at, 64), :] * jnp.exp2(peaks - top[None]), axis=0)
            level = top + jnp.log2(jnp.sum(totals, axis=1, keepdims=True))
            f_scaled[pl.ds(at, 64), :] = log_a[pl.ds(at, 64), :] - relaxed * level
            return carry

        lax.fori_loop(0, rows // 64, some, 0, unroll=2)

    def col_block(block):
        peaks, totals = [], []
        for q in range(rows // LANES):
            at = slice(q * LANES, (q + 1) * LANES)
            x = (scores[block, at, :] + f_scaled[at, :]).reshape(LANES // 8, 8, LANES)
            peak, total = peak_total(x)
            peaks.append(peak)
            totals.append(total)
        top = jnp.max(functools.reduce(jnp.maximum, peaks), axis=0, keepdims=True)
        whole = sum(t * jnp.exp2(p - top) for p, t in zip(peaks, totals))
        return top + jnp.log2(jnp.sum(whole, axis=0, keepdims=True))

    def ex_copy(slot, chunk, step):
        return pltpu.make_async_remote_copy(
            src_ref=parts.at[slot, chunk, me], dst_ref=parts.at[slot, chunk, me],
            send_sem=ex_send.at[slot, chunk, step], recv_sem=ex_recv.at[slot, chunk, me],
            device_id=peer(step), device_id_type=MESH,
        )

    def ex_arrived(slot, chunk, step):
        other = lax.rem(me + step, peers)
        pltpu.make_async_remote_copy(
            src_ref=parts.at[slot, chunk, other], dst_ref=parts.at[slot, chunk, other],
            send_sem=ex_send.at[slot, chunk, 0], recv_sem=ex_recv.at[slot, chunk, other],
            device_id=peer(step), device_id_type=MESH,
        ).wait_recv()

    for chunk in range(chunks):
        row_chunk(chunk)

    def iteration(it, carry):
        slot = lax.rem(it, 2)
        row_finish()
        for chunk in range(chunks):
            for j in range(CHUNK):
                parts[slot, chunk, me, j:j + 1, :] = col_block(chunk * CHUNK + j)
            for step in range(1, peers):
                ex_copy(slot, chunk, step).start()
        for chunk in range(chunks):
            for step in range(1, peers):
                ex_arrived(slot, chunk, step)
            peak, total = peak_total(parts[slot, chunk])
            level = -relaxed * (peak + jnp.log2(total))
            for j in range(CHUNK):
                g_scaled[chunk * CHUNK + j] = (
                    jnp.broadcast_to(level[j:j + 1, :], (8, LANES)) + log_b[chunk * CHUNK + j]
                )
            row_chunk(chunk)
        for chunk in range(chunks):
            for step in range(1, peers):
                ex_copy(slot, chunk, step).wait_send()
        return carry

    lax.fori_loop(0, ITERS, iteration, 0)

    back = entropic * math.log(2.0)
    for k in range(rows // LANES):
        at = slice(k * LANES, (k + 1) * LANES)
        turned = ((f_scaled[at, :] - log_a[at, :]) * back).T
        f_parts[r_id, k:k + 1, :] = turned[0:1, :]

    def f_copy(turn):
        return pltpu.make_async_remote_copy(
            src_ref=f_parts.at[r_id], dst_ref=f_parts.at[r_id],
            send_sem=f_send.at[turn], recv_sem=f_recv.at[r_id],
            device_id={"rep": rep_of(turn)}, device_id_type=MESH,
        )

    for turn in range(1, R):
        f_copy(turn).start()
    for k in range(per):
        at = (c_id * R + r_id) * per + k
        g_ref[k:k + 1, :] = ((g_scaled[at] - log_b[at]) * back)[0:1, :]

    def own_scores(block):
        return scores[block, rows:rows + own, :].reshape(own // 8, 8, LANES) + g_scaled[block][None]

    def own_peak(block, peak):
        return jnp.maximum(peak, own_scores(block))

    peak = lax.fori_loop(1, blocks, own_peak, own_scores(0), unroll=5)
    top = jnp.max(peak, axis=2, keepdims=True)
    for step in range(C):
        for turn in range(R):
            if step or turn:
                ft_arrived(col_of(step), rep_of(turn))

    def fate_block(block, carry):
        total, weighted = carry
        pieces = [jnp.exp2(own_scores(block * per + k) - top) for k in range(per)]
        total = total + sum(pieces)
        weights = jnp.concatenate([p.reshape(own, LANES) for p in pieces], axis=1)
        weighted = weighted + lax.dot_general(
            weights, ft[block // R, lax.rem(block, R)], (((1,), (1,)), ((), ())),
            precision=HIGHEST, preferred_element_type=jnp.float32,
        )
        return total, weighted

    total, weighted = lax.fori_loop(
        0, C * R, fate_block,
        (jnp.zeros((own // 8, 8, LANES), jnp.float32), jnp.zeros((own, fates), jnp.float32)),
    )
    out_ref[...] = weighted / jnp.sum(total.reshape(own, LANES), axis=1, keepdims=True)
    for turn in range(1, R):
        pltpu.make_async_remote_copy(
            src_ref=f_parts.at[rep_of(turn)], dst_ref=f_parts.at[rep_of(turn)],
            send_sem=f_send.at[0], recv_sem=f_recv.at[rep_of(turn)],
            device_id={"rep": rep_of(turn)}, device_id_type=MESH,
        ).wait_recv()
    f_ref[...] = f_parts[...]

    for turn in range(1, R):
        f_copy(turn).wait_send()
        for step in range(C):
            fwd_copy(col_of(step), turn).wait_send()
    for step in range(1, C):
        tt_copy(step).wait_send()
    for step in range(C):
        for turn in range(R):
            if step or turn:
                ft_copy(step, turn).wait_send()


def solution(mesh):
    X, C, R = mesh.shape["rows"], mesh.shape["cols"], mesh.shape["rep"]

    def body(sources, source_mass, targets, target_mass, fate_panel):
        src_count, dim = sources.shape
        tgt_count, fates = fate_panel.shape
        rows, own = src_count // R, src_count // (C * R)
        blocks = C * R * tgt_count // LANES
        chunks = blocks // CHUNK
        peers = X * R
        vmem = pl.BlockSpec(memory_space=pltpu.VMEM)
        dma = pltpu.SemaphoreType.DMA
        f32 = jnp.float32
        f_pot, g_pot, fate_rows = pl.pallas_call(
            functools.partial(kernel, (X, C, R, src_count, tgt_count, dim, fates)),
            out_shape=(
                jax.ShapeDtypeStruct((R, rows // LANES, LANES), f32),
                jax.ShapeDtypeStruct((tgt_count // LANES, LANES), f32),
                jax.ShapeDtypeStruct((own, fates), f32),
            ),
            in_specs=[vmem] * 5,
            out_specs=(vmem,) * 3,
            scratch_shapes=[
                pltpu.VMEM((C, R, dim + 8, tgt_count), f32),
                pltpu.VMEM((C, R, fates, tgt_count), f32),
                pltpu.VMEM((blocks, rows + own, LANES), f32),
                pltpu.VMEM((blocks, 8, LANES), f32),
                pltpu.VMEM((blocks, 8, LANES), f32),
                pltpu.VMEM((rows, LANES), f32),
                pltpu.VMEM((rows, LANES), f32),
                pltpu.VMEM((chunks, rows, LANES), f32),
                pltpu.VMEM((chunks, rows, LANES), f32),
                pltpu.VMEM((2, chunks, peers, CHUNK, LANES), f32),
                pltpu.VMEM((R, rows // LANES, LANES), f32),
                dma((C,)), dma((C,)),
                dma((C, R)), dma((C, R)),
                dma((C, R)), dma((C, R)),
                dma((2, chunks, peers)), dma((2, chunks, peers)),
                dma((R,)), dma((R,)),
            ],
            compiler_params=pltpu.CompilerParams(
                collective_id=0, has_side_effects=True, vmem_limit_bytes=48 * 2**20
            ),
            name="transport",
        )(
            sources,
            source_mass.reshape(R, rows // LANES, LANES),
            targets,
            target_mass.reshape(1, tgt_count),
            fate_panel,
        )
        return f_pot.reshape(src_count), g_pot.reshape(tgt_count), fate_rows

    in_specs = (
        P(("parts", "rows"), None),
        P(("parts", "rows")),
        P(("parts", "cols", "rep"), None),
        P(("parts", "cols", "rep")),
        P(("parts", "cols", "rep"), None),
    )
    out_specs = (
        P(("parts", "rows")),
        P(("parts", "cols", "rep")),
        P(("parts", "rows", "cols", "rep"), None),
    )
    return jax.shard_map(body, mesh=mesh, in_specs=in_specs, out_specs=out_specs, check_vma=False)
```

time: 400 us -> 73.7 us (0.18)
  the two profiles are of different devices: /device:TPU:0 before, /device:TPU:13 now
where the time goes in v1:
time: 73.7 us; the launch traced here: 73.5 us
  Pallas kernels  68.3 us (93%)
  local copies, waits for them, and re-layouts  4.44 us (6%)
    pallas_call x1, Pallas kernels, body(): pl.pallas_call(functools.partial(kernel, (X, C, R, src_count, tgt_count,...  68.3 us
    unnamed x12, local copies, waits for them, and re-layouts  4.44 us

profile of v1, /device:TPU:13, one launch (start us, length us, event | category | flops | bytes accessed | tf_op | source)
XLA Modules:
  0.0 73.5 jit_solution(14288802942329337758)
XLA Ops:
  0.6 0.0 copy-start.2
  0.6 1.0 %copy.9.tgt_ref = f32[256,64]{1,0:T(8,128)S(1)} copy(f32[256,64]{0,1:T(8,128)} %param.7) | data formatting | bytes 131072 | tf_op args[2]
  1.6 0.9 %copy.10.fate_ref = f32[256,64]{1,0:T(8,128)S(1)} copy(f32[256,64]{0,1:T(8,128)} %param.9) | data formatting | bytes 131072 | tf_op args[4]
  2.6 0.0 copy-done.2
  2.6 0.0 copy-start
  2.6 0.0 copy-start.1
  2.6 0.2 copy.8.src_ref
  2.8 0.5 copy-done
  3.3 0.0 copy-done.1
  3.3 68.3 %transport.1 = (f32[2,4,128]{2,1,0:T(4,128)S(1)}, f32[2,128]{1,0:T(2,128)S(1)}, f32[128,64]{1,0:T(8,128)S(1)}) custom-call(f32[1024,64]{1,0:T(8,128)S(1)} %copy.8.src_ref, f32[2,4,128]{2,1,0:T(4,128)S(1)} %bitcast.4, f32[256,64]{1,0:T(8,128)S(1)} %copy.9.tgt_ref, f32[1,256]{1,0:T(1,128)S(1)} %bitcast.6, f32[256,64]{1,0:T(8,128)S(1)} %copy.10.fate_ref), custom_call_target="tpu_custom_call" | custom-call | tf_op jit(solution)/shard_map/transport/pallas_call | solution.py:320
  71.6 0.7 copy.11
  72.3 0.6 copy.14
  72.9 0.6 copy.15
Async XLA Ops:
  0.6 1.9 %copy-start.2 = (f32[1024,64]{0,1:T(8,128)S(1)}, f32[1024,64]{0,1:T(8,128)}, u32[]{:S(2)}) copy-start(f32[1024,64]{0,1:T(8,128)} %param.5) | copy-start | bytes 786436
  2.6 0.7 copy-start
  2.6 0.7 copy-start.1

commit v2 on v1

--- a/solution.py
+++ b/solution.py
@@ -13,8 +13,15 @@
 CHUNK = 8
 entropic = 0.1
 relaxed = 1.0 / 1.1
-HIGHEST = lax.Precision.HIGHEST
 MESH = pl.DeviceIdType.MESH
+
+
+def split(x, pieces):
+    out = []
+    for k in range(pieces):
+        out.append(x.astype(jnp.bfloat16).astype(jnp.float32))
+        x = x - out[-1]
+    return out
 
 
 def peak_total(x):
@@ -26,6 +33,7 @@
     sizes, src_ref, smass_ref, tgt_ref, tmass_ref, fate_ref,
     f_ref, g_ref, out_ref,
     tt, ft, scores, log_b, g_scaled, log_a, f_scaled, row_peak, row_total, parts, f_parts,
+    lhs, src_level,
     tt_send, tt_recv, fwd_send, fwd_recv, ft_send, ft_recv, ex_send, ex_recv, f_send, f_recv,
 ):
     X, C, R, src_count, tgt_count, dim, fates = sizes
@@ -61,11 +69,8 @@
                 device_id_type=MESH,
             )
 
-    both = jnp.concatenate([tgt_ref[...], fate_ref[...]], axis=1)
-    for k in range(per):
-        turned = both[k * LANES:(k + 1) * LANES].T
-        tt[c_id, r_id, 0:dim, k * LANES:(k + 1) * LANES] = turned[:dim]
-        ft[c_id, r_id, :, k * LANES:(k + 1) * LANES] = turned[dim:]
+    tt[c_id, r_id, 0:dim, :] = tgt_ref[...]
+    ft[c_id, r_id, :, :] = fate_ref[...]
     tt[c_id, r_id, dim:dim + 8, :] = jnp.broadcast_to(
         jnp.log2(tmass_ref[...] / all_targets), (8, tgt_count)
     )
@@ -126,16 +131,22 @@
     first = pl.multiple_of(r_id * rows, rows)
     first_own = pl.multiple_of((c_id * R + r_id) * own, own)
     mine = jnp.concatenate([src_ref[pl.ds(first, rows), :], src_ref[pl.ds(first_own, own), :]], axis=0)
-    src_sq = jnp.sum(mine * mine, axis=1, keepdims=True) * unit
-    mine = mine * (2.0 * unit)
+    src_level[...] = jnp.broadcast_to(
+        jnp.sum(mine * mine, axis=1, keepdims=True) * unit, src_level.shape
+    )
+    a, b, c = split(mine * (2.0 * unit), 3)
+    lhs[...] = jnp.concatenate([a, a, b, a, c, b], axis=1).astype(jnp.bfloat16)
 
     def fill(col, rep):
         block = tt[col, rep, 0:dim, :]
-        products = jnp.dot(mine, block, precision=HIGHEST, preferred_element_type=jnp.float32)
-        values = products - (src_sq + jnp.sum(block * block, axis=0, keepdims=True) * unit)
+        a, b, c = [p.astype(jnp.bfloat16) for p in split(block, 3)]
+        rhs = jnp.concatenate([a, b, a, c, a, b], axis=0)
+        products = jnp.dot(lhs[...], rhs, preferred_element_type=jnp.float32)
+        tgt_level = jnp.sum(block * block, axis=0, keepdims=True) * unit
         for k in range(per):
             at = (col * R + rep) * per + k
-            scores[at] = values[:, k * LANES:(k + 1) * LANES]
+            lanes = slice(k * LANES, (k + 1) * LANES)
+            scores[at] = products[:, lanes] - (src_level[...] + tgt_level[:, lanes])
             level = tt[col, rep, dim:dim + 8, k * LANES:(k + 1) * LANES]
             log_b[at] = level
             g_scaled[at] = level
@@ -167,19 +178,14 @@
             row_total[chunk, pl.ds(at, 8), :] = total
             return carry
 
-        lax.fori_loop(0, groups, row_group, 0, unroll=4)
+        lax.fori_loop(0, groups, row_group, 0, unroll=8)
 
     def row_finish():
-        def some(k, carry):
-            at = pl.multiple_of(k * 64, 64)
-            peaks = row_peak[:, pl.ds(at, 64), :]
-            top = jnp.max(jnp.max(peaks, axis=0), axis=1, keepdims=True)
-            totals = jnp.sum(row_total[:, pl.ds(at, 64), :] * jnp.exp2(peaks - top[None]), axis=0)
-            level = top + jnp.log2(jnp.sum(totals, axis=1, keepdims=True))
-            f_scaled[pl.ds(at, 64), :] = log_a[pl.ds(at, 64), :] - relaxed * level
-            return carry
-
-        lax.fori_loop(0, rows // 64, some, 0, unroll=2)
+        peaks = row_peak[...]
+        top = jnp.max(jnp.max(peaks, axis=0), axis=1, keepdims=True)
+        totals = jnp.sum(row_total[...] * jnp.exp2(peaks - top[None]), axis=0)
+        level = top + jnp.log2(jnp.sum(totals, axis=1, keepdims=True))
+        f_scaled[...] = log_a[...] - relaxed * level
 
     def col_block(block):
         peaks, totals = [], []
@@ -268,22 +274,29 @@
             if step or turn:
                 ft_arrived(col_of(step), rep_of(turn))
 
+    def across(left, right):
+        return lax.dot_general(
+            left, right, (((1,), (1,)), ((), ())), preferred_element_type=jnp.float32
+        )
+
     def fate_block(block, carry):
         total, weighted = carry
         pieces = [jnp.exp2(own_scores(block * per + k) - top) for k in range(per)]
         total = total + sum(pieces)
         weights = jnp.concatenate([p.reshape(own, LANES) for p in pieces], axis=1)
-        weighted = weighted + lax.dot_general(
-            weights, ft[block // R, lax.rem(block, R)], (((1,), (1,)), ((), ())),
-            precision=HIGHEST, preferred_element_type=jnp.float32,
-        )
-        return total, weighted
+        high, low = [p.astype(jnp.bfloat16) for p in split(weights, 2)]
+        panel = [p.astype(jnp.bfloat16) for p in split(ft[block // R, lax.rem(block, R)], 2)]
+        return total, weighted + across(high, jnp.concatenate(panel, axis=0)) + across(
+            low, jnp.concatenate([panel[0], jnp.zeros_like(panel[0])], axis=0)
+        )
 
     total, weighted = lax.fori_loop(
         0, C * R, fate_block,
-        (jnp.zeros((own // 8, 8, LANES), jnp.float32), jnp.zeros((own, fates), jnp.float32)),
-    )
-    out_ref[...] = weighted / jnp.sum(total.reshape(own, LANES), axis=1, keepdims=True)
+        (jnp.zeros((own // 8, 8, LANES), jnp.float32), jnp.zeros((own, 2 * fates), jnp.float32)),
+    )
+    weighted = weighted / jnp.sum(total.reshape(own, LANES), axis=1, keepdims=True)
+    turned = weighted.T
+    out_ref[...] = turned[:fates] + turned[fates:]
     for turn in range(1, R):
         pltpu.make_async_remote_copy(
             src_ref=f_parts.at[rep_of(turn)], dst_ref=f_parts.at[rep_of(turn)],
@@ -322,7 +335,7 @@
             out_shape=(
                 jax.ShapeDtypeStruct((R, rows // LANES, LANES), f32),
                 jax.ShapeDtypeStruct((tgt_count // LANES, LANES), f32),
-                jax.ShapeDtypeStruct((own, fates), f32),
+                jax.ShapeDtypeStruct((fates, own), f32),
             ),
             in_specs=[vmem] * 5,
             out_specs=(vmem,) * 3,
@@ -338,6 +351,8 @@
                 pltpu.VMEM((chunks, rows, LANES), f32),
                 pltpu.VMEM((2, chunks, peers, CHUNK, LANES), f32),
                 pltpu.VMEM((R, rows // LANES, LANES), f32),
+                pltpu.VMEM((rows + own, 6 * dim), jnp.bfloat16),
+                pltpu.VMEM((rows + own, LANES), f32),
                 dma((C,)), dma((C,)),
                 dma((C, R)), dma((C, R)),
                 dma((C, R)), dma((C, R)),
@@ -351,11 +366,11 @@
         )(
             sources,
             source_mass.reshape(R, rows // LANES, LANES),
-            targets,
+            targets.T,
             target_mass.reshape(1, tgt_count),
-            fate_panel,
-        )
-        return f_pot.reshape(src_count), g_pot.reshape(tgt_count), fate_rows
+            fate_panel.T,
+        )
+        return f_pot.reshape(src_count), g_pot.reshape(tgt_count), fate_rows.T
 
     in_specs = (
         P(("parts", "rows"), None),

time: 73.7 us -> 61.5 us (0.83)
  the two profiles are of different devices: /device:TPU:13 before, /device:TPU:9 now
where the time goes in v2:
time: 61.5 us; the launch traced here: 61.3 us
  Pallas kernels  57.7 us (94%)
  local copies, waits for them, and re-layouts  2.99 us (5%)
  between operations  0.71 us (1%)
    pallas_call x1, Pallas kernels, body(): pl.pallas_call(functools.partial(kernel, (X, C, R, src_count, tgt_count,...  57.7 us
    unnamed x12, local copies, waits for them, and re-layouts  2.99 us

profile of v2, /device:TPU:9, one launch (start us, length us, event | category | flops | bytes accessed | tf_op | source)
XLA Modules:
  0.0 61.3 jit_solution(1743357218576550075)
XLA Ops:
  0.6 0.0 copy-start
  0.6 0.0 copy-start.1
  0.7 0.0 copy-start.2
  0.7 0.0 copy-start.3
  0.7 1.2 %copy.8.src_ref = f32[1024,64]{1,0:T(8,128)S(1)} copy(f32[1024,64]{0,1:T(8,128)} %param.5) | data formatting | bytes 524288 | tf_op args[0]
  1.9 0.0 copy-done
  1.9 0.0 copy-done.1
  1.9 0.0 copy-done.2
  1.9 0.0 copy-done.3
  1.9 57.7 %transport.1 = (f32[2,4,128]{2,1,0:T(4,128)S(1)}, f32[2,128]{1,0:T(2,128)S(1)}, f32[64,128]{1,0:T(8,128)S(1)}) custom-call(f32[1024,64]{1,0:T(8,128)S(1)} %copy.8.src_ref, f32[2,4,128]{2,1,0:T(4,128)S(1)} %bitcast.10, f32[64,256]{1,0:T(8,128)S(1)} %bitcast.7, f32[1,256]{1,0:T(1,128)S(1)} %bitcast.12, f32[64,256]{1,0:T(8,128)S(1)} %bitcast.8), custom_call_target="tpu_custom_call" | custom-call | tf_op jit(solution)/shard_map/transport/pallas_call | solution.py:333
  59.6 0.6 copy.12
  60.2 0.6 copy.13
  60.7 0.6 %copy.14 = f32[128,64]{0,1:T(8,128)} copy(f32[128,64]{0,1:T(8,128)S(1)} %bitcast.9) | data formatting | bytes 65536
Async XLA Ops:
  0.6 1.2 %copy-start = (f32[256,64]{0,1:T(8,128)S(1)}, f32[256,64]{0,1:T(8,128)}, u32[]{:S(2)}) copy-start(f32[256,64]{0,1:T(8,128)} %param.7) | copy-start | bytes 196612
  0.6 1.2 %copy-start.1 = (f32[256,64]{0,1:T(8,128)S(1)}, f32[256,64]{0,1:T(8,128)}, u32[]{:S(2)}) copy-start(f32[256,64]{0,1:T(8,128)} %param.9) | copy-start | bytes 196612
  0.7 1.2 %copy-start.2 = (f32[1024]{0:T(1024)S(1)}, f32[1024]{0:T(1024)}, u32[]{:S(2)}) copy-start(f32[1024]{0:T(1024)} %param.6) | copy-start | bytes 12292
  0.7 1.2 %copy-start.3 = (f32[256]{0:T(256)S(1)}, f32[256]{0:T(256)}, u32[]{:S(2)}) copy-start(f32[256]{0:T(256)} %param.8) | copy-start | bytes 3076

commit v3 on v2

--- a/solution.py
+++ b/solution.py
@@ -10,6 +10,7 @@
 
 ITERS = 8
 LANES = 128
+PAIR = 2
 CHUNK = 8
 entropic = 0.1
 relaxed = 1.0 / 1.1
@@ -33,25 +34,36 @@
     sizes, src_ref, smass_ref, tgt_ref, tmass_ref, fate_ref,
     f_ref, g_ref, out_ref,
     tt, ft, scores, log_b, g_scaled, log_a, f_scaled, row_peak, row_total, parts, f_parts,
-    lhs, src_level,
+    lhs, src_level, src_rows,
     tt_send, tt_recv, fwd_send, fwd_recv, ft_send, ft_recv, ex_send, ex_recv, f_send, f_recv,
 ):
     X, C, R, src_count, tgt_count, dim, fates = sizes
-    rows = src_count // R
+    rows = src_count // (R * PAIR)
     own = src_count // (C * R)
     blocks = C * R * tgt_count // LANES
     chunks = blocks // CHUNK
     per = tgt_count // LANES
     groups = rows // 8
-    peers = X * R
+    peers = X * PAIR * R
     x_id, c_id, r_id = lax.axis_index("rows"), lax.axis_index("cols"), lax.axis_index("rep")
-    me = x_id * R + r_id
+    c_base = c_id // PAIR * PAIR
+    shares = PAIR * R
+    share = (c_id - c_base) * R + r_id
+    me = x_id * shares + share
     all_sources, all_targets = src_count * X, tgt_count * C * R
     unit = math.log2(math.e) / (dim * entropic)
 
     def peer(step):
         other = lax.rem(me + step, peers)
-        return {"rows": other // R, "rep": lax.rem(other, R)}
+        return {
+            "rows": other // shares,
+            "cols": c_base + lax.rem(other, shares) // R,
+            "rep": lax.rem(other, R),
+        }
+
+    def share_of(step):
+        other = lax.rem(share + step, shares)
+        return {"cols": c_base + other // R, "rep": lax.rem(other, R)}
 
     def col_of(step):
         return lax.rem(c_id + step, C)
@@ -62,12 +74,13 @@
     barrier = pltpu.get_barrier_semaphore()
     for step in range(1, peers):
         pl.semaphore_signal(barrier, inc=1, device_id=peer(step), device_id_type=MESH)
-    for step in range(1, C):
+    for step in range(C):
         for turn in range(R):
-            pl.semaphore_signal(
-                barrier, inc=1, device_id={"cols": col_of(step), "rep": rep_of(turn)},
-                device_id_type=MESH,
-            )
+            if step or turn:
+                pl.semaphore_signal(
+                    barrier, inc=1, device_id={"cols": col_of(step), "rep": rep_of(turn)},
+                    device_id_type=MESH,
+                )
 
     tt[c_id, r_id, 0:dim, :] = tgt_ref[...]
     ft[c_id, r_id, :, :] = fate_ref[...]
@@ -75,7 +88,21 @@
         jnp.log2(tmass_ref[...] / all_targets), (8, tgt_count)
     )
 
-    pl.semaphore_wait(barrier, peers - 1 + (C - 1) * R)
+    for k in range(src_count // LANES):
+        at = slice(k * LANES, (k + 1) * LANES)
+        src_rows[at, :] = src_ref[:, at].T
+    first = pl.multiple_of(share * rows, rows)
+    first_own = pl.multiple_of((c_id * R + r_id) * own, own)
+    mine = jnp.concatenate(
+        [src_rows[pl.ds(first, rows), :], src_rows[pl.ds(first_own, own), :]], axis=0
+    )
+    src_level[...] = jnp.broadcast_to(
+        jnp.sum(mine * mine, axis=1, keepdims=True) * unit, src_level.shape
+    )
+    a, b, c = split(mine * (2.0 * unit), 3)
+    lhs[...] = jnp.concatenate([a, a, b, a, c, b], axis=1).astype(jnp.bfloat16)
+
+    pl.semaphore_wait(barrier, peers - 1 + C * R - 1)
 
     def tt_copy(step):
         return pltpu.make_async_remote_copy(
@@ -127,15 +154,6 @@
         for turn in range(R):
             if step or turn:
                 ft_copy(step, turn).start()
-
-    first = pl.multiple_of(r_id * rows, rows)
-    first_own = pl.multiple_of((c_id * R + r_id) * own, own)
-    mine = jnp.concatenate([src_ref[pl.ds(first, rows), :], src_ref[pl.ds(first_own, own), :]], axis=0)
-    src_level[...] = jnp.broadcast_to(
-        jnp.sum(mine * mine, axis=1, keepdims=True) * unit, src_level.shape
-    )
-    a, b, c = split(mine * (2.0 * unit), 3)
-    lhs[...] = jnp.concatenate([a, a, b, a, c, b], axis=1).astype(jnp.bfloat16)
 
     def fill(col, rep):
         block = tt[col, rep, 0:dim, :]
@@ -153,7 +171,7 @@
 
     fill(c_id, r_id)
     for k in range(rows // LANES):
-        level = jnp.log2(smass_ref[r_id, k:k + 1, :] / all_sources)
+        level = jnp.log2(smass_ref[share, k:k + 1, :] / all_sources)
         log_a[k * LANES:(k + 1) * LANES, :] = jnp.broadcast_to(level, (LANES, LANES)).T
     for turn in range(1, R):
         fwd_arrived(c_id, rep_of(turn))
@@ -246,16 +264,16 @@
     for k in range(rows // LANES):
         at = slice(k * LANES, (k + 1) * LANES)
         turned = ((f_scaled[at, :] - log_a[at, :]) * back).T
-        f_parts[r_id, k:k + 1, :] = turned[0:1, :]
+        f_parts[share, k:k + 1, :] = turned[0:1, :]
 
     def f_copy(turn):
         return pltpu.make_async_remote_copy(
-            src_ref=f_parts.at[r_id], dst_ref=f_parts.at[r_id],
-            send_sem=f_send.at[turn], recv_sem=f_recv.at[r_id],
-            device_id={"rep": rep_of(turn)}, device_id_type=MESH,
-        )
-
-    for turn in range(1, R):
+            src_ref=f_parts.at[share], dst_ref=f_parts.at[share],
+            send_sem=f_send.at[turn], recv_sem=f_recv.at[share],
+            device_id=share_of(turn), device_id_type=MESH,
+        )
+
+    for turn in range(1, shares):
         f_copy(turn).start()
     for k in range(per):
         at = (c_id * R + r_id) * per + k
@@ -297,16 +315,18 @@
     weighted = weighted / jnp.sum(total.reshape(own, LANES), axis=1, keepdims=True)
     turned = weighted.T
     out_ref[...] = turned[:fates] + turned[fates:]
-    for turn in range(1, R):
+    for turn in range(1, shares):
+        other = lax.rem(share + turn, shares)
         pltpu.make_async_remote_copy(
-            src_ref=f_parts.at[rep_of(turn)], dst_ref=f_parts.at[rep_of(turn)],
-            send_sem=f_send.at[0], recv_sem=f_recv.at[rep_of(turn)],
-            device_id={"rep": rep_of(turn)}, device_id_type=MESH,
+            src_ref=f_parts.at[other], dst_ref=f_parts.at[other],
+            send_sem=f_send.at[0], recv_sem=f_recv.at[other],
+            device_id=share_of(turn), device_id_type=MESH,
         ).wait_recv()
     f_ref[...] = f_parts[...]
 
+    for turn in range(1, shares):
+        f_copy(turn).wait_send()
     for turn in range(1, R):
-        f_copy(turn).wait_send()
         for step in range(C):
             fwd_copy(col_of(step), turn).wait_send()
     for step in range(1, C):
@@ -323,17 +343,18 @@
     def body(sources, source_mass, targets, target_mass, fate_panel):
         src_count, dim = sources.shape
         tgt_count, fates = fate_panel.shape
-        rows, own = src_count // R, src_count // (C * R)
+        shares = PAIR * R
+        rows, own = src_count // shares, src_count // (C * R)
         blocks = C * R * tgt_count // LANES
         chunks = blocks // CHUNK
-        peers = X * R
+        peers = X * shares
         vmem = pl.BlockSpec(memory_space=pltpu.VMEM)
         dma = pltpu.SemaphoreType.DMA
         f32 = jnp.float32
         f_pot, g_pot, fate_rows = pl.pallas_call(
             functools.partial(kernel, (X, C, R, src_count, tgt_count, dim, fates)),
             out_shape=(
-                jax.ShapeDtypeStruct((R, rows // LANES, LANES), f32),
+                jax.ShapeDtypeStruct((shares, rows // LANES, LANES), f32),
                 jax.ShapeDtypeStruct((tgt_count // LANES, LANES), f32),
                 jax.ShapeDtypeStruct((fates, own), f32),
             ),
@@ -350,22 +371,23 @@
                 pltpu.VMEM((chunks, rows, LANES), f32),
                 pltpu.VMEM((chunks, rows, LANES), f32),
                 pltpu.VMEM((2, chunks, peers, CHUNK, LANES), f32),
-                pltpu.VMEM((R, rows // LANES, LANES), f32),
+                pltpu.VMEM((shares, rows // LANES, LANES), f32),
                 pltpu.VMEM((rows + own, 6 * dim), jnp.bfloat16),
                 pltpu.VMEM((rows + own, LANES), f32),
+                pltpu.VMEM((src_count, dim), f32),
                 dma((C,)), dma((C,)),
                 dma((C, R)), dma((C, R)),
                 dma((C, R)), dma((C, R)),
                 dma((2, chunks, peers)), dma((2, chunks, peers)),
-                dma((R,)), dma((R,)),
+                dma((shares,)), dma((shares,)),
             ],
             compiler_params=pltpu.CompilerParams(
                 collective_id=0, has_side_effects=True, vmem_limit_bytes=48 * 2**20
             ),
             name="transport",
         )(
-            sources,
-            source_mass.reshape(R, rows // LANES, LANES),
+            sources.T,
+            source_mass.reshape(shares, rows // LANES, LANES),
             targets.T,
             target_mass.reshape(1, tgt_count),
             fate_panel.T,

time: 61.5 us -> 64.2 us (1.044)
  the two profiles are of different devices: /device:TPU:9 before, /device:TPU:0 now
where the time goes in v3:
time: 64.2 us; the launch traced here: 63.9 us
  Pallas kernels  58.1 us (90%)
  local copies, waits for them, and re-layouts  5.08 us (8%)
  between operations  0.66 us (1%)
    pallas_call x1, Pallas kernels, body(): pl.pallas_call(functools.partial(kernel, (X, C, R, src_count, tgt_count,...  58.1 us
    unnamed x13, local copies, waits for them, and re-layouts  5.08 us

profile of v3, /device:TPU:0, one launch (start us, length us, event | category | flops | bytes accessed | tf_op | source)
XLA Modules:
  0.0 63.9 jit_solution(17209894040647013317)
XLA Ops:
  0.6 0.0 copy-start.3
  0.6 0.0 copy-start.4
  0.7 0.7 %copy-done.3 = f32[1024]{0:T(1024)S(1)} copy-done((f32[1024]{0:T(1024)S(1)}, f32[1024]{0:T(1024)}, u32[]{:S(2)}) %copy-start.3) | copy-done | bytes 4120
  1.3 0.0 copy-done.4
  1.3 0.0 copy-start
  1.3 0.9 %copy-done = f32[1024,64]{0,1:T(8,128)S(1)} copy-done((f32[1024,64]{0,1:T(8,128)S(1)}, f32[1024,64]{0,1:T(8,128)}, u32[]{:S(2)}) %copy-start) | copy-done | bytes 262168
  2.3 0.0 copy-start.1
  2.3 0.8 %copy-done.1 = f32[256,64]{0,1:T(8,128)S(1)} copy-done((f32[256,64]{0,1:T(8,128)S(1)}, f32[256,64]{0,1:T(8,128)}, u32[]{:S(2)}) %copy-start.1) | copy-done | bytes 65560
  3.1 0.0 copy-start.2
  3.1 0.8 %copy-done.2 = f32[256,64]{0,1:T(8,128)S(1)} copy-done((f32[256,64]{0,1:T(8,128)S(1)}, f32[256,64]{0,1:T(8,128)}, u32[]{:S(2)}) %copy-start.2) | copy-done | bytes 65560
  4.0 58.1 %transport.1 = (f32[4,2,128]{2,1,0:T(2,128)S(1)}, f32[2,128]{1,0:T(2,128)S(1)}, f32[64,128]{1,0:T(8,128)S(1)}) custom-call(f32[64,1024]{1,0:T(8,128)S(1)} %bitcast.8, f32[4,2,128]{2,1,0:T(2,128)S(1)} %bitcast.12, f32[64,256]{1,0:T(8,128)S(1)} %bitcast.9, f32[1,256]{1,0:T(1,128)S(1)} %bitcast.14, f32[64,256]{1,0:T(8,128)S(1)} %bitcast.10), custom_call_target="tpu_custom_call" | custom-call | tf_op jit(solution)/shard_map/transport/pallas_call | solution.py:354
  62.1 0.6 copy.11
  62.7 0.6 copy.12
  63.3 0.6 copy.13
Async XLA Ops:
  0.6 0.7 %copy-start.3 = (f32[1024]{0:T(1024)S(1)}, f32[1024]{0:T(1024)}, u32[]{:S(2)}) copy-start(f32[1024]{0:T(1024)} %param.6) | copy-start | bytes 12292
  0.6 0.7 %copy-start.4 = (f32[256]{0:T(256)S(1)}, f32[256]{0:T(256)}, u32[]{:S(2)}) copy-start(f32[256]{0:T(256)} %param.8) | copy-start | bytes 3076
  1.3 0.9 %copy-start = (f32[1024,64]{0,1:T(8,128)S(1)}, f32[1024,64]{0,1:T(8,128)}, u32[]{:S(2)}) copy-start(f32[1024,64]{0,1:T(8,128)} %param.5) | copy-start | bytes 786436
  2.3 0.8 %copy-start.1 = (f32[256,64]{0,1:T(8,128)S(1)}, f32[256,64]{0,1:T(8,128)}, u32[]{:S(2)}) copy-start(f32[256,64]{0,1:T(8,128)} %param.7) | copy-start | bytes 196612
  3.1 0.8 %copy-start.2 = (f32[256,64]{0,1:T(8,128)S(1)}, f32[256,64]{0,1:T(8,128)}, u32[]{:S(2)}) copy-start(f32[256,64]{0,1:T(8,128)} %param.9) | copy-start | bytes 196612

commit v4 on v3

--- a/solution.py
+++ b/solution.py
@@ -10,7 +10,7 @@
 
 ITERS = 8
 LANES = 128
-PAIR = 2
+PAIR = 1
 CHUNK = 8
 entropic = 0.1
 relaxed = 1.0 / 1.1
@@ -43,6 +43,7 @@
     blocks = C * R * tgt_count // LANES
     chunks = blocks // CHUNK
     per = tgt_count // LANES
+    width = CHUNK // (R * per)
     groups = rows // 8
     peers = X * PAIR * R
     x_id, c_id, r_id = lax.axis_index("rows"), lax.axis_index("cols"), lax.axis_index("rep")
@@ -169,6 +170,57 @@
             log_b[at] = level
             g_scaled[at] = level
 
+    def row_chunk(chunk):
+        base = chunk * CHUNK
+        g_chunk = g_scaled[pl.ds(base, CHUNK)]
+
+        def row_group(group, carry):
+            at = pl.multiple_of(group * 8, 8)
+            x = scores[pl.ds(base, CHUNK), pl.ds(at, 8), :] + g_chunk
+            peak, total = peak_total(x)
+            row_peak[chunk, pl.ds(at, 8), :] = peak
+            row_total[chunk, pl.ds(at, 8), :] = total
+            return carry
+
+        lax.fori_loop(0, groups, row_group, 0, unroll=8)
+
+    def row_finish():
+        peaks = row_peak[...]
+        top = jnp.max(jnp.max(peaks, axis=0), axis=1, keepdims=True)
+        totals = jnp.sum(row_total[...] * jnp.exp2(peaks - top[None]), axis=0)
+        level = top + jnp.log2(jnp.sum(totals, axis=1, keepdims=True))
+        f_scaled[...] = log_a[...] - relaxed * level
+
+    def col_blocks(blocks):
+        peaks, totals = [[] for b in blocks], [[] for b in blocks]
+        for q in range(rows // LANES):
+            at = slice(q * LANES, (q + 1) * LANES)
+            f_rows = f_scaled[at, :]
+            for k, block in enumerate(blocks):
+                x = (scores[block, at, :] + f_rows).reshape(LANES // 8, 8, LANES)
+                peak, total = peak_total(x)
+                peaks[k].append(peak)
+                totals[k].append(total)
+        for k in range(len(blocks)):
+            top = jnp.max(functools.reduce(jnp.maximum, peaks[k]), axis=0, keepdims=True)
+            whole = sum(t * jnp.exp2(p - top) for p, t in zip(peaks[k], totals[k]))
+            yield top + jnp.log2(jnp.sum(whole, axis=0, keepdims=True))
+
+    def ex_copy(slot, chunk, step):
+        return pltpu.make_async_remote_copy(
+            src_ref=parts.at[slot, chunk, me], dst_ref=parts.at[slot, chunk, me],
+            send_sem=ex_send.at[slot, chunk, step], recv_sem=ex_recv.at[slot, chunk, me],
+            device_id=peer(step), device_id_type=MESH,
+        )
+
+    def ex_arrived(slot, chunk, step):
+        other = lax.rem(me + step, peers)
+        pltpu.make_async_remote_copy(
+            src_ref=parts.at[slot, chunk, other], dst_ref=parts.at[slot, chunk, other],
+            send_sem=ex_send.at[slot, chunk, 0], recv_sem=ex_recv.at[slot, chunk, other],
+            device_id=peer(step), device_id_type=MESH,
+        ).wait_recv()
+
     fill(c_id, r_id)
     for k in range(rows // LANES):
         level = jnp.log2(smass_ref[share, k:k + 1, :] / all_sources)
@@ -176,71 +228,35 @@
     for turn in range(1, R):
         fwd_arrived(c_id, rep_of(turn))
         fill(c_id, rep_of(turn))
-    for step in range(1, C):
-        tt_arrived(col_of(step))
-        for turn in range(1, R):
-            fwd_copy(col_of(step), turn).start()
-        fill(col_of(step), r_id)
-    for step in range(1, C):
-        for turn in range(1, R):
-            fwd_arrived(col_of(step), rep_of(turn))
-            fill(col_of(step), rep_of(turn))
-
-    def row_chunk(chunk):
-        def row_group(group, carry):
-            at = pl.multiple_of(group * 8, 8)
-            base = chunk * CHUNK
-            x = scores[pl.ds(base, CHUNK), pl.ds(at, 8), :] + g_scaled[pl.ds(base, CHUNK)]
-            peak, total = peak_total(x)
-            row_peak[chunk, pl.ds(at, 8), :] = peak
-            row_total[chunk, pl.ds(at, 8), :] = total
-            return carry
-
-        lax.fori_loop(0, groups, row_group, 0, unroll=8)
-
-    def row_finish():
-        peaks = row_peak[...]
-        top = jnp.max(jnp.max(peaks, axis=0), axis=1, keepdims=True)
-        totals = jnp.sum(row_total[...] * jnp.exp2(peaks - top[None]), axis=0)
-        level = top + jnp.log2(jnp.sum(totals, axis=1, keepdims=True))
-        f_scaled[...] = log_a[...] - relaxed * level
-
-    def col_block(block):
-        peaks, totals = [], []
-        for q in range(rows // LANES):
-            at = slice(q * LANES, (q + 1) * LANES)
-            x = (scores[block, at, :] + f_scaled[at, :]).reshape(LANES // 8, 8, LANES)
-            peak, total = peak_total(x)
-            peaks.append(peak)
-            totals.append(total)
-        top = jnp.max(functools.reduce(jnp.maximum, peaks), axis=0, keepdims=True)
-        whole = sum(t * jnp.exp2(p - top) for p, t in zip(peaks, totals))
-        return top + jnp.log2(jnp.sum(whole, axis=0, keepdims=True))
-
-    def ex_copy(slot, chunk, step):
-        return pltpu.make_async_remote_copy(
-            src_ref=parts.at[slot, chunk, me], dst_ref=parts.at[slot, chunk, me],
-            send_sem=ex_send.at[slot, chunk, step], recv_sem=ex_recv.at[slot, chunk, me],
-            device_id=peer(step), device_id_type=MESH,
-        )
-
-    def ex_arrived(slot, chunk, step):
-        other = lax.rem(me + step, peers)
-        pltpu.make_async_remote_copy(
-            src_ref=parts.at[slot, chunk, other], dst_ref=parts.at[slot, chunk, other],
-            send_sem=ex_send.at[slot, chunk, 0], recv_sem=ex_recv.at[slot, chunk, other],
-            device_id=peer(step), device_id_type=MESH,
-        ).wait_recv()
-
-    for chunk in range(chunks):
-        row_chunk(chunk)
+    ready = None
+    for p in range(chunks):
+        chunk = lax.rem(c_id // width + p, chunks)
+        if p:
+            cols = [chunk * width + k for k in range(width)]
+        else:
+            cols = [chunk * width + lax.rem(c_id + k, width) for k in range(1, width)]
+        for col in cols:
+            tt_arrived(col)
+            for turn in range(1, R):
+                fwd_copy(col, turn).start()
+            fill(col, r_id)
+        if ready is not None:
+            row_chunk(ready)
+        for col in cols:
+            for turn in range(1, R):
+                fwd_arrived(col, rep_of(turn))
+                fill(col, rep_of(turn))
+        ready = chunk
+    row_chunk(ready)
 
     def iteration(it, carry):
         slot = lax.rem(it, 2)
         row_finish()
         for chunk in range(chunks):
-            for j in range(CHUNK):
-                parts[slot, chunk, me, j:j + 1, :] = col_block(chunk * CHUNK + j)
+            levels = []
+            for j in range(0, CHUNK, 2):
+                levels += col_blocks([chunk * CHUNK + j, chunk * CHUNK + j + 1])
+            parts[slot, chunk, me] = jnp.concatenate(levels, axis=0)
             for step in range(1, peers):
                 ex_copy(slot, chunk, step).start()
         for chunk in range(chunks):

time: 64.2 us -> 62.4 us (0.972)
  the two profiles are of different devices: /device:TPU:0 before, /device:TPU:9 now
where the time goes in v4:
time: 62.4 us; the launch traced here: 62.1 us
  Pallas kernels  56.4 us (90%)
  local copies, waits for them, and re-layouts  5.08 us (8%)
  between operations  0.66 us (1%)
    pallas_call x1, Pallas kernels, body(): pl.pallas_call(functools.partial(kernel, (X, C, R, src_count, tgt_count,...  56.4 us
    unnamed x13, local copies, waits for them, and re-layouts  5.08 us

profile of v4, /device:TPU:9, one launch (start us, length us, event | category | flops | bytes accessed | tf_op | source)
XLA Modules:
  0.0 62.1 jit_solution(11921604320409123902)
XLA Ops:
  0.6 0.0 copy-start.3
  0.6 0.0 copy-start.4
  0.7 0.7 %copy-done.3 = f32[1024]{0:T(1024)S(1)} copy-done((f32[1024]{0:T(1024)S(1)}, f32[1024]{0:T(1024)}, u32[]{:S(2)}) %copy-start.3) | copy-done | bytes 4120
  1.3 0.0 copy-done.4
  1.3 0.0 copy-start
  1.3 0.9 %copy-done = f32[1024,64]{0,1:T(8,128)S(1)} copy-done((f32[1024,64]{0,1:T(8,128)S(1)}, f32[1024,64]{0,1:T(8,128)}, u32[]{:S(2)}) %copy-start) | copy-done | bytes 262168
  2.3 0.0 copy-start.1
  2.3 0.8 %copy-done.1 = f32[256,64]{0,1:T(8,128)S(1)} copy-done((f32[256,64]{0,1:T(8,128)S(1)}, f32[256,64]{0,1:T(8,128)}, u32[]{:S(2)}) %copy-start.1) | copy-done | bytes 65560
  3.1 0.0 copy-start.2
  3.1 0.8 %copy-done.2 = f32[256,64]{0,1:T(8,128)S(1)} copy-done((f32[256,64]{0,1:T(8,128)S(1)}, f32[256,64]{0,1:T(8,128)}, u32[]{:S(2)}) %copy-start.2) | copy-done | bytes 65560
  4.0 56.4 %transport.1 = (f32[2,4,128]{2,1,0:T(4,128)S(1)}, f32[2,128]{1,0:T(2,128)S(1)}, f32[64,128]{1,0:T(8,128)S(1)}) custom-call(f32[64,1024]{1,0:T(8,128)S(1)} %bitcast.8, f32[2,4,128]{2,1,0:T(4,128)S(1)} %bitcast.12, f32[64,256]{1,0:T(8,128)S(1)} %bitcast.9, f32[1,256]{1,0:T(1,128)S(1)} %bitcast.14, f32[64,256]{1,0:T(8,128)S(1)} %bitcast.10), custom_call_target="tpu_custom_call" | custom-call | tf_op jit(solution)/shard_map/transport/pallas_call | solution.py:370
  60.4 0.6 copy.11
  60.9 0.6 copy.12
  61.5 0.6 copy.13
Async XLA Ops:
  0.6 0.7 %copy-start.3 = (f32[1024]{0:T(1024)S(1)}, f32[1024]{0:T(1024)}, u32[]{:S(2)}) copy-start(f32[1024]{0:T(1024)} %param.6) | copy-start | bytes 12292
  0.6 0.7 %copy-start.4 = (f32[256]{0:T(256)S(1)}, f32[256]{0:T(256)}, u32[]{:S(2)}) copy-start(f32[256]{0:T(256)} %param.8) | copy-start | bytes 3076
  1.3 0.9 %copy-start = (f32[1024,64]{0,1:T(8,128)S(1)}, f32[1024,64]{0,1:T(8,128)}, u32[]{:S(2)}) copy-start(f32[1024,64]{0,1:T(8,128)} %param.5) | copy-start | bytes 786436
  2.3 0.8 %copy-start.1 = (f32[256,64]{0,1:T(8,128)S(1)}, f32[256,64]{0,1:T(8,128)}, u32[]{:S(2)}) copy-start(f32[256,64]{0,1:T(8,128)} %param.7) | copy-start | bytes 196612
  3.1 0.8 %copy-start.2 = (f32[256,64]{0,1:T(8,128)S(1)}, f32[256,64]{0,1:T(8,128)}, u32[]{:S(2)}) copy-start(f32[256,64]{0,1:T(8,128)} %param.9) | copy-start | bytes 196612

commit v5 on v4

--- a/solution.py
+++ b/solution.py
@@ -89,6 +89,54 @@
         jnp.log2(tmass_ref[...] / all_targets), (8, tgt_count)
     )
 
+    pl.semaphore_wait(barrier, peers - 1 + C * R - 1)
+
+    def tt_copy(step):
+        return pltpu.make_async_remote_copy(
+            src_ref=tt.at[c_id, r_id], dst_ref=tt.at[c_id, r_id],
+            send_sem=tt_send.at[step], recv_sem=tt_recv.at[c_id],
+            device_id={"cols": col_of(step)}, device_id_type=MESH,
+        )
+
+    def fwd_copy(col, turn):
+        return pltpu.make_async_remote_copy(
+            src_ref=tt.at[col, r_id], dst_ref=tt.at[col, r_id],
+            send_sem=fwd_send.at[col, turn], recv_sem=fwd_recv.at[col, r_id],
+            device_id={"rep": rep_of(turn)}, device_id_type=MESH,
+        )
+
+    def ft_copy(step, turn):
+        return pltpu.make_async_remote_copy(
+            src_ref=ft.at[c_id, r_id], dst_ref=ft.at[c_id, r_id],
+            send_sem=ft_send.at[step, turn], recv_sem=ft_recv.at[c_id, r_id],
+            device_id={"cols": col_of(step), "rep": rep_of(turn)}, device_id_type=MESH,
+        )
+
+    def tt_arrived(col):
+        pltpu.make_async_remote_copy(
+            src_ref=tt.at[col, r_id], dst_ref=tt.at[col, r_id],
+            send_sem=tt_send.at[0], recv_sem=tt_recv.at[col],
+            device_id={"cols": col}, device_id_type=MESH,
+        ).wait_recv()
+
+    def fwd_arrived(col, rep):
+        pltpu.make_async_remote_copy(
+            src_ref=tt.at[col, rep], dst_ref=tt.at[col, rep],
+            send_sem=fwd_send.at[col, 0], recv_sem=fwd_recv.at[col, rep],
+            device_id={"rep": rep}, device_id_type=MESH,
+        ).wait_recv()
+
+    def ft_arrived(col, rep):
+        pltpu.make_async_remote_copy(
+            src_ref=ft.at[col, rep], dst_ref=ft.at[col, rep],
+            send_sem=ft_send.at[0, 0], recv_sem=ft_recv.at[col, rep],
+            device_id={"cols": col, "rep": rep}, device_id_type=MESH,
+        ).wait_recv()
+
+    for step in range(1, C):
+        tt_copy(step).start()
+    for turn in range(1, R):
+        fwd_copy(c_id, turn).start()
     for k in range(src_count // LANES):
         at = slice(k * LANES, (k + 1) * LANES)
         src_rows[at, :] = src_ref[:, at].T
@@ -103,58 +151,6 @@
     a, b, c = split(mine * (2.0 * unit), 3)
     lhs[...] = jnp.concatenate([a, a, b, a, c, b], axis=1).astype(jnp.bfloat16)
 
-    pl.semaphore_wait(barrier, peers - 1 + C * R - 1)
-
-    def tt_copy(step):
-        return pltpu.make_async_remote_copy(
-            src_ref=tt.at[c_id, r_id], dst_ref=tt.at[c_id, r_id],
-            send_sem=tt_send.at[step], recv_sem=tt_recv.at[c_id],
-            device_id={"cols": col_of(step)}, device_id_type=MESH,
-        )
-
-    def fwd_copy(col, turn):
-        return pltpu.make_async_remote_copy(
-            src_ref=tt.at[col, r_id], dst_ref=tt.at[col, r_id],
-            send_sem=fwd_send.at[col, turn], recv_sem=fwd_recv.at[col, r_id],
-            device_id={"rep": rep_of(turn)}, device_id_type=MESH,
-        )
-
-    def ft_copy(step, turn):
-        return pltpu.make_async_remote_copy(
-            src_ref=ft.at[c_id, r_id], dst_ref=ft.at[c_id, r_id],
-            send_sem=ft_send.at[step, turn], recv_sem=ft_recv.at[c_id, r_id],
-            device_id={"cols": col_of(step), "rep": rep_of(turn)}, device_id_type=MESH,
-        )
-
-    def tt_arrived(col):
-        pltpu.make_async_remote_copy(
-            src_ref=tt.at[col, r_id], dst_ref=tt.at[col, r_id],
-            send_sem=tt_send.at[0], recv_sem=tt_recv.at[col],
-            device_id={"cols": col}, device_id_type=MESH,
-        ).wait_recv()
-
-    def fwd_arrived(col, rep):
-        pltpu.make_async_remote_copy(
-            src_ref=tt.at[col, rep], dst_ref=tt.at[col, rep],
-            send_sem=fwd_send.at[col, 0], recv_sem=fwd_recv.at[col, rep],
-            device_id={"rep": rep}, device_id_type=MESH,
-        ).wait_recv()
-
-    def ft_arrived(col, rep):
-        pltpu.make_async_remote_copy(
-            src_ref=ft.at[col, rep], dst_ref=ft.at[col, rep],
-            send_sem=ft_send.at[0, 0], recv_sem=ft_recv.at[col, rep],
-            device_id={"cols": col, "rep": rep}, device_id_type=MESH,
-        ).wait_recv()
-
-    for step in range(1, C):
-        tt_copy(step).start()
-    for turn in range(1, R):
-        fwd_copy(c_id, turn).start()
-    for step in list(range(1, C)) + [0]:
-        for turn in range(R):
-            if step or turn:
-                ft_copy(step, turn).start()
 
     def fill(col, rep):
         block = tt[col, rep, 0:dim, :]
@@ -247,6 +243,10 @@
                 fwd_arrived(col, rep_of(turn))
                 fill(col, rep_of(turn))
         ready = chunk
+    for step in list(range(1, C)) + [0]:
+        for turn in range(R):
+            if step or turn:
+                ft_copy(step, turn).start()
     row_chunk(ready)
 
     def iteration(it, carry):

time: 62.4 us -> 57.7 us (0.925)
  the two profiles are of different devices: /device:TPU:9 before, /device:TPU:0 now
where the time goes in v5:
time: 57.7 us; the launch traced here: 57.4 us
  Pallas kernels  51.7 us (90%)
  local copies, waits for them, and re-layouts  5.08 us (9%)
  between operations  0.66 us (1%)
    pallas_call x1, Pallas kernels, body(): pl.pallas_call(functools.partial(kernel, (X, C, R, src_count, tgt_count,...  51.7 us
    unnamed x13, local copies, waits for them, and re-layouts  5.08 us

profile of v5, /device:TPU:0, one launch (start us, length us, event | category | flops | bytes accessed | tf_op | source)
XLA Modules:
  0.0 57.4 jit_solution(595609423072394827)
XLA Ops:
  0.6 0.0 copy-start.3
  0.6 0.0 copy-start.4
  0.7 0.7 %copy-done.3 = f32[1024]{0:T(1024)S(1)} copy-done((f32[1024]{0:T(1024)S(1)}, f32[1024]{0:T(1024)}, u32[]{:S(2)}) %copy-start.3) | copy-done | bytes 4120
  1.3 0.0 copy-done.4
  1.3 0.0 copy-start
  1.3 0.9 %copy-done = f32[1024,64]{0,1:T(8,128)S(1)} copy-done((f32[1024,64]{0,1:T(8,128)S(1)}, f32[1024,64]{0,1:T(8,128)}, u32[]{:S(2)}) %copy-start) | copy-done | bytes 262168
  2.3 0.0 copy-start.1
  2.3 0.8 %copy-done.1 = f32[256,64]{0,1:T(8,128)S(1)} copy-done((f32[256,64]{0,1:T(8,128)S(1)}, f32[256,64]{0,1:T(8,128)}, u32[]{:S(2)}) %copy-start.1) | copy-done | bytes 65560
  3.1 0.0 copy-start.2
  3.1 0.8 %copy-done.2 = f32[256,64]{0,1:T(8,128)S(1)} copy-done((f32[256,64]{0,1:T(8,128)S(1)}, f32[256,64]{0,1:T(8,128)}, u32[]{:S(2)}) %copy-start.2) | copy-done | bytes 65560
  4.0 51.7 %transport.1 = (f32[2,4,128]{2,1,0:T(4,128)S(1)}, f32[2,128]{1,0:T(2,128)S(1)}, f32[64,128]{1,0:T(8,128)S(1)}) custom-call(f32[64,1024]{1,0:T(8,128)S(1)} %bitcast.8, f32[2,4,128]{2,1,0:T(4,128)S(1)} %bitcast.12, f32[64,256]{1,0:T(8,128)S(1)} %bitcast.9, f32[1,256]{1,0:T(1,128)S(1)} %bitcast.14, f32[64,256]{1,0:T(8,128)S(1)} %bitcast.10), custom_call_target="tpu_custom_call" | custom-call | tf_op jit(solution)/shard_map/transport/pallas_call | solution.py:370
  55.7 0.6 %copy.11 = f32[1024]{0:T(1024)} copy(f32[1024]{0:T(1024)S(1)} %bitcast.13) | data formatting | bytes 8192
  56.3 0.6 copy.12
  56.8 0.6 %copy.13 = f32[128,64]{0,1:T(8,128)} copy(f32[128,64]{0,1:T(8,128)S(1)} %bitcast.11) | data formatting | bytes 65536
Async XLA Ops:
  0.6 0.7 %copy-start.3 = (f32[1024]{0:T(1024)S(1)}, f32[1024]{0:T(1024)}, u32[]{:S(2)}) copy-start(f32[1024]{0:T(1024)} %param.6) | copy-start | bytes 12292
  0.6 0.7 %copy-start.4 = (f32[256]{0:T(256)S(1)}, f32[256]{0:T(256)}, u32[]{:S(2)}) copy-start(f32[256]{0:T(256)} %param.8) | copy-start | bytes 3076
  1.3 0.9 %copy-start = (f32[1024,64]{0,1:T(8,128)S(1)}, f32[1024,64]{0,1:T(8,128)}, u32[]{:S(2)}) copy-start(f32[1024,64]{0,1:T(8,128)} %param.5) | copy-start | bytes 786436
  2.3 0.8 %copy-start.1 = (f32[256,64]{0,1:T(8,128)S(1)}, f32[256,64]{0,1:T(8,128)}, u32[]{:S(2)}) copy-start(f32[256,64]{0,1:T(8,128)} %param.7) | copy-start | bytes 196612
  3.1 0.8 %copy-start.2 = (f32[256,64]{0,1:T(8,128)S(1)}, f32[256,64]{0,1:T(8,128)}, u32[]{:S(2)}) copy-start(f32[256,64]{0,1:T(8,128)} %param.9) | copy-start | bytes 196612

commit v6 on v5

--- a/solution.py
+++ b/solution.py
@@ -31,10 +31,10 @@
 
 
 def kernel(
-    sizes, src_ref, smass_ref, tgt_ref, tmass_ref, fate_ref,
+    sizes, src_hbm, smass_hbm, tgt_hbm, tmass_hbm, fate_hbm,
     f_ref, g_ref, out_ref,
     tt, ft, scores, log_b, g_scaled, log_a, f_scaled, row_peak, row_total, parts, f_parts,
-    lhs, src_level, src_rows,
+    lhs, src_level, src_rows, src_ref, smass_ref, tmass_ref, in_sem,
     tt_send, tt_recv, fwd_send, fwd_recv, ft_send, ft_recv, ex_send, ex_recv, f_send, f_recv,
 ):
     X, C, R, src_count, tgt_count, dim, fates = sizes
@@ -72,6 +72,18 @@
     def rep_of(step):
         return lax.rem(r_id + step, R)
 
+    loads = [
+        pltpu.make_async_copy(origin, target, in_sem.at[k])
+        for k, (origin, target) in enumerate([
+            (tgt_hbm, tt.at[c_id, r_id, pl.ds(0, dim)]),
+            (tmass_hbm, tmass_ref),
+            (src_hbm, src_ref),
+            (smass_hbm, smass_ref),
+            (fate_hbm, ft.at[c_id, r_id]),
+        ])
+    ]
+    for load in loads:
+        load.start()
     barrier = pltpu.get_barrier_semaphore()
     for step in range(1, peers):
         pl.semaphore_signal(barrier, inc=1, device_id=peer(step), device_id_type=MESH)
@@ -83,12 +95,12 @@
                     device_id_type=MESH,
                 )
 
-    tt[c_id, r_id, 0:dim, :] = tgt_ref[...]
-    ft[c_id, r_id, :, :] = fate_ref[...]
+    loads[1].wait()
     tt[c_id, r_id, dim:dim + 8, :] = jnp.broadcast_to(
         jnp.log2(tmass_ref[...] / all_targets), (8, tgt_count)
     )
 
+    loads[0].wait()
     pl.semaphore_wait(barrier, peers - 1 + C * R - 1)
 
     def tt_copy(step):
@@ -137,6 +149,7 @@
         tt_copy(step).start()
     for turn in range(1, R):
         fwd_copy(c_id, turn).start()
+    loads[2].wait()
     for k in range(src_count // LANES):
         at = slice(k * LANES, (k + 1) * LANES)
         src_rows[at, :] = src_ref[:, at].T
@@ -218,6 +231,7 @@
         ).wait_recv()
 
     fill(c_id, r_id)
+    loads[3].wait()
     for k in range(rows // LANES):
         level = jnp.log2(smass_ref[share, k:k + 1, :] / all_sources)
         log_a[k * LANES:(k + 1) * LANES, :] = jnp.broadcast_to(level, (LANES, LANES)).T
@@ -243,6 +257,7 @@
                 fwd_arrived(col, rep_of(turn))
                 fill(col, rep_of(turn))
         ready = chunk
+    loads[4].wait()
     for step in list(range(1, C)) + [0]:
         for turn in range(R):
             if step or turn:
@@ -374,7 +389,7 @@
                 jax.ShapeDtypeStruct((tgt_count // LANES, LANES), f32),
                 jax.ShapeDtypeStruct((fates, own), f32),
             ),
-            in_specs=[vmem] * 5,
+            in_specs=[pl.BlockSpec(memory_space=pltpu.HBM)] * 5,
             out_specs=(vmem,) * 3,
             scratch_shapes=[
                 pltpu.VMEM((C, R, dim + 8, tgt_count), f32),
@@ -391,6 +406,10 @@
                 pltpu.VMEM((rows + own, 6 * dim), jnp.bfloat16),
                 pltpu.VMEM((rows + own, LANES), f32),
                 pltpu.VMEM((src_count, dim), f32),
+                pltpu.VMEM((dim, src_count), f32),
+                pltpu.VMEM((shares, rows // LANES, LANES), f32),
+                pltpu.VMEM((1, tgt_count), f32),
+                dma((5,)),
                 dma((C,)), dma((C,)),
                 dma((C, R)), dma((C, R)),
                 dma((C, R)), dma((C, R)),

time: 57.7 us -> 58 us (level)
  no operation moved by 1% of the time
where the time goes in v6:
time: 58 us; the launch traced here: 57.7 us
  Pallas kernels  52 us (90%)
  local copies, waits for them, and re-layouts  5.08 us (9%)
  between operations  0.66 us (1%)
    pallas_call x1, Pallas kernels, body(): pl.pallas_call(functools.partial(kernel, (X, C, R, src_count, tgt_count,...  52 us
    unnamed x13, local copies, waits for them, and re-layouts  5.08 us

profile of v6, /device:TPU:0, one launch (start us, length us, event | category | flops | bytes accessed | tf_op | source)
XLA Modules:
  0.0 57.7 jit_solution(5507002135047655954)
XLA Ops:
  0.6 0.0 copy-start.3
  0.6 0.0 copy-start.4
  0.7 0.7 %copy-done.3 = f32[1024]{0:T(1024)S(1)} copy-done((f32[1024]{0:T(1024)S(1)}, f32[1024]{0:T(1024)}, u32[]{:S(2)}) %copy-start.3) | copy-done | bytes 4120
  1.3 0.0 copy-done.4
  1.3 0.0 copy-start
  1.3 0.9 %copy-done = f32[1024,64]{0,1:T(8,128)S(1)} copy-done((f32[1024,64]{0,1:T(8,128)S(1)}, f32[1024,64]{0,1:T(8,128)}, u32[]{:S(2)}) %copy-start) | copy-done | bytes 262168
  2.3 0.0 copy-start.1
  2.3 0.8 %copy-done.1 = f32[256,64]{0,1:T(8,128)S(1)} copy-done((f32[256,64]{0,1:T(8,128)S(1)}, f32[256,64]{0,1:T(8,128)}, u32[]{:S(2)}) %copy-start.1) | copy-done | bytes 65560
  3.1 0.0 copy-start.2
  3.1 0.8 %copy-done.2 = f32[256,64]{0,1:T(8,128)S(1)} copy-done((f32[256,64]{0,1:T(8,128)S(1)}, f32[256,64]{0,1:T(8,128)}, u32[]{:S(2)}) %copy-start.2) | copy-done | bytes 65560
  4.0 52.0 %transport.1 = (f32[2,4,128]{2,1,0:T(4,128)S(1)}, f32[2,128]{1,0:T(2,128)S(1)}, f32[64,128]{1,0:T(8,128)S(1)}) custom-call(f32[64,1024]{1,0:T(8,128)S(1)} %bitcast.8, f32[2,4,128]{2,1,0:T(4,128)S(1)} %bitcast.12, f32[64,256]{1,0:T(8,128)S(1)} %bitcast.9, f32[1,256]{1,0:T(1,128)S(1)} %bitcast.14, f32[64,256]{1,0:T(8,128)S(1)} %bitcast.10), custom_call_target="tpu_custom_call" | custom-call | tf_op jit(solution)/shard_map/transport/pallas_call | solution.py:385
  55.9 0.6 %copy.11 = f32[1024]{0:T(1024)} copy(f32[1024]{0:T(1024)S(1)} %bitcast.13) | data formatting | bytes 8192
  56.5 0.6 copy.12
  57.1 0.6 %copy.13 = f32[128,64]{0,1:T(8,128)} copy(f32[128,64]{0,1:T(8,128)S(1)} %bitcast.11) | data formatting | bytes 65536
Async XLA Ops:
  0.6 0.7 %copy-start.3 = (f32[1024]{0:T(1024)S(1)}, f32[1024]{0:T(1024)}, u32[]{:S(2)}) copy-start(f32[1024]{0:T(1024)} %param.6) | copy-start | bytes 12292
  0.6 0.7 %copy-start.4 = (f32[256]{0:T(256)S(1)}, f32[256]{0:T(256)}, u32[]{:S(2)}) copy-start(f32[256]{0:T(256)} %param.8) | copy-start | bytes 3076
  1.3 0.9 %copy-start = (f32[1024,64]{0,1:T(8,128)S(1)}, f32[1024,64]{0,1:T(8,128)}, u32[]{:S(2)}) copy-start(f32[1024,64]{0,1:T(8,128)} %param.5) | copy-start | bytes 786436
  2.3 0.8 %copy-start.1 = (f32[256,64]{0,1:T(8,128)S(1)}, f32[256,64]{0,1:T(8,128)}, u32[]{:S(2)}) copy-start(f32[256,64]{0,1:T(8,128)} %param.7) | copy-start | bytes 196612
  3.1 0.8 %copy-start.2 = (f32[256,64]{0,1:T(8,128)S(1)}, f32[256,64]{0,1:T(8,128)}, u32[]{:S(2)}) copy-start(f32[256,64]{0,1:T(8,128)} %param.9) | copy-start | bytes 196612
